TPU v7x, 128 devices: a whole 4x4x4 slice. The times are simulated.
128 devices in a mesh: sec: 4 (over z), dev: 32 (over x, y, core).
Axes of the slice: x: 4, y: 4, z: 4, core: 2. Of those that a mesh axis runs over, the one named last changes fastest.
Arguments:
- tokens: bfloat16 [4096, 3584], P(('sec', 'dev')), may hold values from -6 to 6
- expert_ids: int32 [4096, 8], P(('sec', 'dev')), may hold values from 0 to 127, all different within a row; in each aligned block of 32 rows (0 to 31, 32 to 63, ...) at most 4 rows name the same one
- gate_values: float32 [4096, 8], P(('sec', 'dev')), may hold values from 0.1 to 0.6
- w_gate: bfloat16 [128, 3584, 1024], P(('sec', 'dev')), may hold values from -0.09375 to 0.09375
- w_up: bfloat16 [128, 3584, 1024], P(('sec', 'dev')), may hold values from -0.09375 to 0.09375
- w_down: bfloat16 [128, 1024, 3584], P(('sec', 'dev')), may hold values from -0.1875 to 0.1875
Outputs:
- expert_out: bfloat16 [4096, 3584], P(('sec', 'dev'))
Inputs may be any that keep to these rules, and one draw needn't show every extreme that they name: `expert_ids`: each row names 8 different experts; in the rows of one device no expert is named by more than 4 rows, a bound that some block reaches.
All inputs are finite; a program needn't handle non-finite values.
Results may differ from a plain program's by a relative error of at most 0.0057.
Values may be sent and summed in bfloat16 or wider, within the bound.
A program may use at most 128 MiB of HBM per device.

v0:
```python
import jax
import jax.numpy as jnp
from jax import lax
from jax.sharding import PartitionSpec as P


def expert_answer(rows, w_gate, w_up, w_down):
    shape_in = rows.shape
    flat_rows = rows.reshape(-1, shape_in[-1])
    first = jnp.dot(flat_rows, w_gate[0], preferred_element_type=jnp.float32)
    second = jnp.dot(flat_rows, w_up[0], preferred_element_type=jnp.float32)
    hidden = (jax.nn.silu(first) * second).astype(jnp.bfloat16)
    answer = jnp.dot(hidden, w_down[0], preferred_element_type=jnp.float32).astype(jnp.bfloat16)
    return answer.reshape(shape_in)


def per_device(tokens, expert_ids, gate_values, w_gate, w_up, w_down):
    tok_count, per_token = expert_ids.shape
    width = tokens.shape[1]
    sections = lax.axis_size("sec")
    members = lax.axis_size("dev")
    experts_all = sections * members
    capacity = max(4, 2 * tok_count * per_token // experts_all)
    flat_ids = expert_ids.reshape(-1)
    onehot = (flat_ids[:, None] == jnp.arange(experts_all, dtype=jnp.int32)[None, :]).astype(
        jnp.int32
    )
    before = jnp.cumsum(onehot, axis=0) - onehot
    slot_of = jnp.sum(before * onehot, axis=1)
    target = flat_ids * capacity + slot_of
    source_rows = jnp.repeat(tokens, per_token, axis=0)
    outgoing = jnp.zeros((experts_all * capacity, width), jnp.bfloat16).at[target].set(source_rows)
    answers = expert_answer(
        lax.all_to_all(
            outgoing.reshape(experts_all, capacity, width),
            ("sec", "dev"),
            split_axis=0,
            concat_axis=0,
            tiled=True,
        ),
        w_gate,
        w_up,
        w_down,
    )
    returned = lax.all_to_all(answers, ("sec", "dev"), split_axis=0, concat_axis=0, tiled=True)
    back_rows = returned.reshape(experts_all * capacity, width)[target].reshape(
        tok_count, per_token, width
    )
    expert_out = jnp.sum(gate_values[:, :, None] * back_rows.astype(jnp.float32), axis=1).astype(
        jnp.bfloat16
    )
    return expert_out


def solution(mesh):
    in_specs = (
        P(("sec", "dev"), None),
        P(("sec", "dev"), None),
        P(("sec", "dev"), None),
        P(("sec", "dev"), None, None),
        P(("sec", "dev"), None, None),
        P(("sec", "dev"), None, None),
    )
    out_specs = P(("sec", "dev"), None)
    return jax.shard_map(
        per_device, mesh=mesh, in_specs=in_specs, out_specs=out_specs, check_vma=False
    )
```

profile of v0, /device:TPU:1, one launch (start us, length us, event | category | flops | bytes accessed | tf_op | source)
XLA Modules:
  0.0 179.0 jit_solution(6895142326246441025)
XLA Ops:
  0.0 0.0 copy-start
  0.0 0.8 copy.10
  0.8 0.1 eq.29
  0.9 0.1 eq.25
  1.0 0.7 broadcast_multiply_fusion
  1.7 0.1 copy.12
  1.8 0.2 fusion.18
  2.1 0.1 copy.9
  2.2 0.1 mul.37
  2.3 0.2 fusion.20
  2.5 0.0 copy-done
  2.5 5.5 %scatter_custom_fusion = bf16[512,3584]{1,0:T(8,128)(2,1)} fusion(s32[256]{0:T(256)S(1)} %bitcast.42, bf16[]{:T(256)} %constant.6.clone.1, bf16[32,3584]{1,0:T(8,128)(2,1)S(1)} %copy-done), kind=kCustom, calls=%fused_computation.12 | custom fusion | bytes 3899394 | tf_op jit(solution)/shard_map/scatter | solution.py:32
  7.9 7.0 %reshape.67 = bf16[128,4,3584]{2,1,0:T(4,128)(2,1)} reshape(bf16[512,3584]{1,0:T(8,128)(2,1)} %scatter_custom_fusion) | data formatting | bytes 7340032 | tf_op jit(solution)/shard_map/reshape | solution.py:35
  15.0 59.2 %all_to_all.10 = bf16[128,4,3584]{2,1,0:T(4,128)(2,1)} all-to-all(bf16[128,4,3584]{2,1,0:T(4,128)(2,1)} %reshape.67), channel_id=1, replica_groups=mesh['sec'=4,'dev'=32] {'sec','dev'}, dimensions={0} | all-to-all | bytes 7340032 | tf_op jit(solution)/shard_map/all_to_all | solution.py:34
  74.1 6.7 %reshape.68 = bf16[512,3584]{1,0:T(8,128)(2,1)} reshape(bf16[128,4,3584]{2,1,0:T(4,128)(2,1)} %all_to_all.10) | data formatting | bytes 7340032 | tf_op jit(solution)/shard_map/reshape | solution.py:9
  80.9 7.3 %fusion.2 = f32[512,1024]{1,0:T(8,128)S(1)} fusion(bf16[512,3584]{1,0:T(8,128)(2,1)} %reshape.68, bf16[1,3584,1024]{2,1,0:T(8,128)(2,1)} %param.10), kind=kOutput, calls=%fused_computation.4 | convolution fusion | flops 3758096384 | bytes 13107200 | tf_op jit(solution)/shard_map/dot_general | solution.py:11
  88.2 16.0 %fusion.6 = bf16[512,3584]{1,0:T(8,128)(2,1)} fusion(bf16[1,1024,3584]{2,1,0:T(8,128)(2,1)} %param.11, f32[512,1024]{1,0:T(8,128)S(1)} %fusion.2, bf16[512,3584]{1,0:T(8,128)(2,1)} %reshape.68, bf16[1,3584,1024]{2,1,0:T(8,128)(2,1)} %param.9), kind=kOutput, calls=%fused_computation.8 | convolution fusion | flops 7521173504 | bytes 24117248 | tf_op jit(solution)/shard_map/dot_general | solution.py:13
  104.2 7.0 %reshape.69 = bf16[128,4,3584]{2,1,0:T(4,128)(2,1)} reshape(bf16[512,3584]{1,0:T(8,128)(2,1)} %fusion.6) | data formatting | bytes 7340032 | tf_op jit(solution)/shard_map/reshape | solution.py:14
  111.2 0.0 copy-start.1
  111.2 5.5 %all-to-all-start.1 = ((bf16[128,4,3584]{2,1,0:T(4,128)(2,1)}), bf16[128,4,3584]{2,1,0:T(4,128)(2,1)}, u32[]{:S(2)}, u32[]{:S(2)}) async-start(bf16[128,4,3584]{2,1,0:T(4,128)(2,1)} %reshape.69), calls=%async_computation.1 | async-start | bytes 7340032 | tf_op jit(solution)/shard_map/all_to_all | solution.py:45
  116.7 0.0 copy-done.1
  116.7 0.1 copy.8
  116.7 47.3 %all-to-all-done.1 = bf16[128,4,3584]{2,1,0:T(4,128)(2,1)} async-done(((bf16[128,4,3584]{2,1,0:T(4,128)(2,1)}), bf16[128,4,3584]{2,1,0:T(4,128)(2,1)}, u32[]{:S(2)}, u32[]{:S(2)}) %all-to-all-start.1) | async-done | bytes 3670048 | tf_op jit(solution)/shard_map/all_to_all | solution.py:45
  164.0 6.7 %reshape.70 = bf16[512,3584]{1,0:T(8,128)(2,1)} reshape(bf16[128,4,3584]{2,1,0:T(4,128)(2,1)} %all-to-all-done.1) | data formatting | bytes 7340032 | tf_op jit(solution)/shard_map/reshape | solution.py:46
  170.8 6.0 %gather_fusion = bf16[256,3584]{1,0:T(8,128)(2,1)S(1)} fusion(bf16[512,3584]{1,0:T(8,128)(2,1)} %reshape.70, s32[1024]{0:T(1024)S(1)} %pad_clamp_fusion), kind=kCustom, calls=%fused_computation | custom fusion | bytes 3671040 | tf_op jit(solution)/shard_map/gather | solution.py:46
  176.8 2.1 %fusion.9 = bf16[32,3584]{1,0:T(8,128)(2,1)} fusion(bf16[256,3584]{1,0:T(8,128)(2,1)S(1)} %gather_fusion, f32[32,8]{1,0:T(8,128)S(1)} %copy.8), kind=kLoop, calls=%fused_computation.10 | loop fusion | flops 2637824 | bytes 2065408 | tf_op jit(solution)/shard_map/reduce_sum | solution.py:49
  (8 shorter events, 0.1 us)
Async XLA Ops:
  0.0 2.5 %copy-start = (bf16[32,3584]{1,0:T(8,128)(2,1)S(1)}, bf16[32,3584]{1,0:T(8,128)(2,1)}, u32[]{:S(2)}) copy-start(bf16[32,3584]{1,0:T(8,128)(2,1)} %param.6) | copy-start | bytes 688132
  111.2 5.5 %copy-start.1 = (f32[32,8]{0,1:T(8,128)S(1)}, f32[32,8]{0,1:T(8,128)}, u32[]{:S(2)}) copy-start(f32[32,8]{0,1:T(8,128)} %param.8) | copy-start | bytes 3076
  111.2 52.8 %all-to-all-start.1 = ((bf16[128,4,3584]{2,1,0:T(4,128)(2,1)}), bf16[128,4,3584]{2,1,0:T(4,128)(2,1)}, u32[]{:S(2)}, u32[]{:S(2)}) async-start(bf16[128,4,3584]{2,1,0:T(4,128)(2,1)} %reshape.69), calls=%async_computation.1 | async-start | bytes 7340032 | tf_op jit(solution)/shard_map/all_to_all | solution.py:45
where the time goes:
time: 180 us; the launch traced here: 179 us
  blocking collectives  59.2 us (33%)
  waiting for transfers between devices  47.3 us (26%)
  local copies, waits for them, and re-layouts  40.4 us (22%)
  matrix products  23.3 us (13%)
  starting transfers between devices  5.45 us (3%)
  other arithmetic  3.28 us (2%)
    all_to_all x1, blocking collectives, per_device(): lax.all_to_all(outgoing.reshape(experts_all, capacity, width), ('sec', 'd...  59.2 us
    all_to_all x1, waiting for transfers between devices, per_device(): lax.all_to_all(answers, ('sec', 'dev'), split_axis=0, concat_axis=0, tile...  47.3 us
    dot_general x1, matrix products, expert_answer(): jnp.dot(hidden, w_down[0], preferred_element_type=jnp.float32)  16 us
    dot_general x1, matrix products, expert_answer(): second = jnp.dot(flat_rows, w_up[0], preferred_element_type=jnp.float32)  7.3 us
    reshape x1, local copies, waits for them, and re-layouts, per_device(): outgoing.reshape(experts_all, capacity, width)  7 us
    reshape x1, local copies, waits for them, and re-layouts, expert_answer(): return answer.reshape(shape_in)  7 us
    reshape x1, local copies, waits for them, and re-layouts, per_device(): returned.reshape(experts_all * capacity, width)[target]  6.75 us
    reshape x1, local copies, waits for them, and re-layouts, expert_answer(): flat_rows = rows.reshape(-1, shape_in[-1])  6.74 us
  transfers between devices with their start and end apart: 1, of which 1 were waited for; matrix products, arithmetic and copies ran while one was open for 0% of the time, Pallas kernels for 0%

commit v1 on v0

v1 whole, which is shorter than its diff:
```python
import jax
import jax.numpy as jnp
from jax import lax
from jax.experimental import pallas as pl
from jax.experimental.pallas import tpu as pltpu
from jax.sharding import PartitionSpec as P

MESH = pl.DeviceIdType.MESH
BF = jnp.bfloat16
F32 = jnp.float32
TOK = 32
ROWS = 512
LINE = 128
D = 3584
FF = 1024
ROUNDS = ((512, 384, 384), (384, 384, 512), (384, 384, 256))


def chunks():
    out, start = [], 0
    for widths in ROUNDS:
        row = []
        for width in widths:
            row.append((start, width))
            start += width
        out.append(row)
    return out


def coords():
    z, d = lax.axis_index("sec"), lax.axis_index("dev")
    return z, lax.div(d, 8), lax.rem(lax.div(d, 2), 4), lax.rem(d, 2)


def plane_split(p, co):
    z, x, y, _ = co
    return ((x, y, z), (z, y, x), (z, x, y))[p]


def device_of(p, u, v, j, c):
    z, x, y = ((j, u, v), (u, j, v), (u, v, j))[p]
    return (z, x * 8 + y * 2 + c)


def plane_peer(p, co, n):
    u, v, j = plane_split(p, co)
    un = lax.rem(u + lax.div(n, 8), 4)
    vn = lax.rem(v + lax.rem(lax.div(n, 2), 4), 4)
    cn = lax.rem(co[3] + n, 2)
    return device_of(p, un, vn, j, cn), un * 8 + vn * 2 + cn


def line_peer(p, co, n):
    u, v, j = plane_split(p, co)
    jn = lax.rem(j + n, 4)
    return device_of(p, u, v, jn, co[3]), jn


def iota(shape, dim):
    return lax.broadcasted_iota(jnp.int32, shape, dim)


def dot_nt(a, b):
    return lax.dot_general(a, b, (((1,), (1,)), ((), ())), preferred_element_type=F32)


def dot(a, b):
    return jnp.dot(a, b, preferred_element_type=F32)


def plane_experts(p, co, shape):
    e = lax.shift_right_logical(iota(shape, 0), 4)
    uv, c = lax.shift_right_logical(e, 1), e & 1
    u, v = lax.shift_right_logical(uv, 2), uv & 3
    _, _, j = plane_split(p, co)
    z, x, y = ((j, u, v), (u, j, v), (u, v, j))[p]
    expert = z * 32 + x * 8 + y * 2 + c
    return (iota(shape, 1) == expert).astype(F32).astype(BF)


def reorder(p):
    shape = (ROWS, ROWS)
    r = iota(shape, 0)
    slot, z = r & 3, lax.shift_right_logical(r, 2) & 3
    c, y = lax.shift_right_logical(r, 4) & 1, lax.shift_right_logical(r, 5) & 3
    x = lax.shift_right_logical(r, 7)
    u, v, j = plane_split(p, (z, x, y, c))
    other = (u * 8 + v * 2 + c) * 16 + j * 4 + slot
    return (iota(shape, 1) == other).astype(F32).astype(BF)


def wait_for(ref, sem):
    pltpu.make_async_copy(ref, ref, sem).wait()


def kernel(
    ids_ref, gates_ref, tok_ref, wg_hbm, wu_hbm, wd_hbm, out_ref,
    wg, wu, wd, meta, metas, gath, send, recv, acc_g, acc_u, hid, ans, back, part, fin,
    perm, pick, comb,
    w_sem, meta_ss, meta_rs, s1_ss, s1_rs, s2_ss, s2_rs, s4_ss, s4_rs, s5_ss, s5_rs,
):
    co = coords()
    table = chunks()

    barrier = pltpu.get_barrier_semaphore()
    for p in range(3):
        u, v, j = plane_split(p, co)

        def greet(n, carry, p=p):
            du, dv = lax.div(n, 8), lax.rem(lax.div(n, 2), 4)
            peer, _ = plane_peer(p, co, n)
            if p == 0:
                pl.semaphore_signal(barrier, inc=1, device_id=peer, device_id_type=MESH)
            else:
                fresh = (du != 0) if p == 1 else (du != 0) & (dv != 0)

                @pl.when(fresh)
                def _():
                    pl.semaphore_signal(barrier, inc=1, device_id=peer, device_id_type=MESH)

            return carry

        lax.fori_loop(1, 32, greet, 0)

    weights = [
        pltpu.make_async_copy(src.at[0], dst, w_sem.at[i])
        for i, (src, dst) in enumerate(((wg_hbm, wg), (wu_hbm, wu), (wd_hbm, wd)))
    ]
    for copy in weights:
        copy.start()

    lanes = iota((TOK, 128), 1)
    named = jnp.zeros((TOK, 128), F32)
    gate = jnp.zeros((TOK, 128), F32)
    for k in range(8):
        hit = ids_ref[:, k : k + 1] == lanes
        named = named + hit.astype(F32)
        gate = gate + jnp.where(hit, gates_ref[:, k : k + 1], 0.0)
    earlier = (iota((TOK, TOK), 1) < iota((TOK, TOK), 0)).astype(F32).astype(BF)
    slot = dot(earlier, named.astype(BF))
    gate_hi = gate.astype(BF)
    meta[:, 0:128] = (named * (slot + 1.0)).astype(BF)
    meta[:, 128:256] = gate_hi
    meta[:, 256:384] = (gate - gate_hi.astype(F32)).astype(BF)

    pl.semaphore_wait(barrier, 73)

    for p in range(3):
        _, _, j = plane_split(p, co)
        mine = pl.ds(pl.multiple_of(j * TOK, TOK), TOK)
        pltpu.make_async_copy(meta, metas.at[p, mine], meta_rs.at[p]).start()
        for n in (1, 3, 2):
            peer, _ = line_peer(p, co, n)
            pltpu.make_async_remote_copy(
                meta, metas.at[p, mine], meta_ss, meta_rs.at[p], device_id=peer, device_id_type=MESH
            ).start()
    for r, row in enumerate(table):
        for p, (start, width) in enumerate(row):
            _, _, j = plane_split(p, co)
            mine = pl.ds(pl.multiple_of(j * TOK, TOK), TOK)
            cols = pl.ds(start, width)
            pltpu.make_async_copy(tok_ref.at[:, cols], gath.at[mine, cols], s1_rs.at[r, p]).start()
            for n in (1, 3, 2):
                peer, _ = line_peer(p, co, n)
                pltpu.make_async_remote_copy(
                    tok_ref.at[:, cols], gath.at[mine, cols], s1_ss, s1_rs.at[r, p],
                    device_id=peer, device_id_type=MESH,
                ).start()

    for p in range(3):
        wait_for(metas.at[p], meta_rs.at[p])
        one = plane_experts(p, co, (ROWS, 128))
        code = metas[p, :, 0:128]
        rows, cols = iota((ROWS, LINE), 0), iota((ROWS, LINE), 1)
        want = ((rows & 3) + 1).astype(F32)
        same = (lax.shift_right_logical(rows, 2) & 3) == lax.shift_right_logical(cols, 5)
        pick[p] = jnp.where((dot_nt(one, code) == want) & same, 1.0, 0.0).astype(BF)

    def plane_send(r, src, dst, ss, rs):
        def body(i, carry):
            n = lax.rem(i * 13, 32)
            for p, (start, width) in enumerate(table[r]):
                cols = pl.ds(start, width)
                u, v, _ = plane_split(p, co)
                me = u * 8 + v * 2 + co[3]
                peer, s = plane_peer(p, co, n)
                pltpu.make_async_remote_copy(
                    src.at[pl.ds(pl.multiple_of(s * 16, 16), 16), cols],
                    dst.at[pl.ds(pl.multiple_of(me * 16, 16), 16), cols],
                    ss, rs.at[r, p], device_id=peer, device_id_type=MESH,
                ).start()
            return carry

        lax.fori_loop(1, 32, body, 0)
        for p, (start, width) in enumerate(table[r]):
            u, v, _ = plane_split(p, co)
            mine = pl.ds(pl.multiple_of((u * 8 + v * 2 + co[3]) * 16, 16), 16)
            cols = pl.ds(start, width)
            pltpu.make_async_copy(src.at[mine, cols], dst.at[mine, cols], rs.at[r, p]).start()

    for r, row in enumerate(table):
        for p, (start, width) in enumerate(row):
            cols = pl.ds(start, width)
            wait_for(gath.at[:, cols], s1_rs.at[r, p])
            send[:, cols] = dot(pick[p], gath[:, cols]).astype(BF)
        plane_send(r, send, recv, s2_ss, s2_rs)

    for p in range(3):
        one = plane_experts(p, co, (ROWS, 128))
        rows, cols = iota((LINE, ROWS), 0), iota((LINE, ROWS), 1)
        want = ((cols & 3) + 1).astype(F32)
        same = (lax.shift_right_logical(cols, 2) & 3) == lax.shift_right_logical(rows, 5)
        hit = (dot_nt(metas[p, :, 0:128], one) == want) & same
        comb[p, 0:LINE] = jnp.where(hit, dot_nt(metas[p, :, 128:256], one), 0.0).astype(BF)
        comb[p, LINE : 2 * LINE] = jnp.where(hit, dot_nt(metas[p, :, 256:384], one), 0.0).astype(BF)
    for p in (1, 2):
        perm[p - 1] = reorder(p)

    for copy in weights:
        copy.wait()

    for r, row in enumerate(table):
        for p, (start, width) in enumerate(row):
            cols = pl.ds(start, width)
            wait_for(recv.at[:, cols], s2_rs.at[r, p])
            if p > 0:
                recv[:, cols] = dot(perm[p - 1], recv[:, cols]).astype(BF)
        first = row[0][0]
        depth = pl.ds(first, sum(width for _, width in row))

        def body(i, carry, r=r, depth=depth):
            at = pl.ds(pl.multiple_of(i * 256, 256), 256)
            g = dot(recv[:, depth], wg[depth, at])
            u = dot(recv[:, depth], wu[depth, at])
            if r > 0:
                g = g + acc_g[:, at]
                u = u + acc_u[:, at]
            if r < len(table) - 1:
                acc_g[:, at] = g
                acc_u[:, at] = u
            else:
                hid[0, :, at] = (g / (1.0 + jnp.exp(-g)) * u).astype(BF)
            return carry

        lax.fori_loop(0, FF // 256, body, 0)
    for p in (1, 2):
        hid[p] = lax.dot_general(
            perm[p - 1], hid[0], (((0,), (0,)), ((), ())), preferred_element_type=F32
        ).astype(BF)

    for r, row in enumerate(table):
        for p, (start, width) in enumerate(row):
            cols = pl.ds(start, width)
            ans[:, cols] = dot(hid[p], wd[:, cols]).astype(BF)
        plane_send(r, ans, back, s4_ss, s4_rs)

    for r, row in enumerate(table):
        for p, (start, width) in enumerate(row):
            _, _, j = plane_split(p, co)
            cols = pl.ds(start, width)
            wait_for(back.at[:, cols], s4_rs.at[r, p])
            both = dot(comb[p], back[:, cols])
            part[:, cols] = (both[0:LINE] + both[LINE : 2 * LINE]).astype(BF)
            for n in (1, 3, 2):
                peer, jn = line_peer(p, co, n)
                pltpu.make_async_remote_copy(
                    part.at[pl.ds(pl.multiple_of(jn * TOK, TOK), TOK), cols], fin.at[j, :, cols],
                    s5_ss, s5_rs.at[r, p], device_id=peer, device_id_type=MESH,
                ).start()
            mine = pl.ds(pl.multiple_of(j * TOK, TOK), TOK)
            pltpu.make_async_copy(part.at[mine, cols], fin.at[j, :, cols], s5_rs.at[r, p]).start()

    for r, row in enumerate(table):
        for p, (start, width) in enumerate(row):
            cols = pl.ds(start, width)
            wait_for(fin.at[:, :, cols], s5_rs.at[r, p])
            total = fin[0, :, cols].astype(F32)
            for k in range(1, 4):
                total = total + fin[k, :, cols].astype(F32)
            out_ref[:, cols] = total.astype(BF)

    wait_for(metas.at[:, pl.ds(0, 96)], meta_ss)
    wait_for(gath.at[pl.ds(0, 96)], s1_ss)
    wait_for(send.at[pl.ds(0, 496)], s2_ss)
    wait_for(ans.at[pl.ds(0, 496)], s4_ss)
    wait_for(part.at[pl.ds(0, 96)], s5_ss)


def per_device(tokens, expert_ids, gate_values, w_gate, w_up, w_down):
    n = len(ROUNDS)
    dma = pltpu.SemaphoreType.DMA
    vmem = pl.BlockSpec(memory_space=pltpu.VMEM)
    hbm = pl.BlockSpec(memory_space=pl.ANY)
    return pl.pallas_call(
        kernel,
        out_shape=jax.ShapeDtypeStruct((TOK, D), BF),
        in_specs=[vmem, vmem, vmem, hbm, hbm, hbm],
        out_specs=vmem,
        scratch_shapes=[
            pltpu.VMEM((D, FF), BF),
            pltpu.VMEM((D, FF), BF),
            pltpu.VMEM((FF, D), BF),
            pltpu.VMEM((TOK, 384), BF),
            pltpu.VMEM((3, LINE, 384), BF),
            pltpu.VMEM((LINE, D), BF),
            pltpu.VMEM((ROWS, D), BF),
            pltpu.VMEM((ROWS, D), BF),
            pltpu.VMEM((ROWS, FF), F32),
            pltpu.VMEM((ROWS, FF), F32),
            pltpu.VMEM((3, ROWS, FF), BF),
            pltpu.VMEM((ROWS, D), BF),
            pltpu.VMEM((ROWS, D), BF),
            pltpu.VMEM((LINE, D), BF),
            pltpu.VMEM((4, TOK, D), BF),
            pltpu.VMEM((2, ROWS, ROWS), BF),
            pltpu.VMEM((3, ROWS, LINE), BF),
            pltpu.VMEM((3, 2 * LINE, ROWS), BF),
            dma((3,)),
            dma, dma((3,)),
            dma, dma((n, 3)),
            dma, dma((n, 3)),
            dma, dma((n, 3)),
            dma, dma((n, 3)),
        ],
        compiler_params=pltpu.CompilerParams(
            collective_id=0, has_side_effects=True, vmem_limit_bytes=60 * 2**20
        ),
        cost_estimate=pl.CostEstimate(
            flops=6 * ROWS * D * FF, bytes_accessed=6 * D * FF, transcendentals=ROWS * FF
        ),
        name="expert_layer",
    )(expert_ids, gate_values, tokens, w_gate, w_up, w_down)


def solution(mesh):
    rows = P(("sec", "dev"), None)
    experts = P(("sec", "dev"), None, None)
    return jax.shard_map(
        per_device,
        mesh=mesh,
        in_specs=(rows, rows, rows, experts, experts, experts),
        out_specs=rows,
        check_vma=False,
    )
```

time: 180 us -> 94.3 us (0.52)
  Pallas kernels: 0 us -> 89.7 us
  blocking collectives: 59.2 us -> 0 us
  waiting for transfers between devices: 47.3 us -> 0 us
  local copies, waits for them, and re-layouts: 40.4 us -> 4.37 us
  matrix products: 23.3 us -> 0 us
  starting transfers between devices: 5.45 us -> 0 us
  other arithmetic: 3.28 us -> 0 us
    pallas_call x0 -> x1, Pallas kernels: none -> 89.7 us  [per_device(): pl.pallas_call(kernel, out_shape=jax.ShapeDtypeStruct((TOK, D), BF), in_s...]
    all_to_all x1 -> x0, blocking collectives: 59.2 us -> none  [per_device(): lax.all_to_all(outgoing.reshape(experts_all, capacity, width), ('sec', 'd...]
    all_to_all x1 -> x0, waiting for transfers between devices: 47.3 us -> none  [per_device(): lax.all_to_all(answers, ('sec', 'dev'), split_axis=0, concat_axis=0, tile...]
    reshape x4 -> x0, local copies, waits for them, and re-layouts: 27.5 us -> none  [the longest x1 7 us: per_device(): outgoing.reshape(experts_all, capacity, width)]
    dot_general x2 -> x0, matrix products: 23.3 us -> none  [the longest x1 16 us: expert_answer(): jnp.dot(hidden, w_down[0], preferred_element_type=jnp.float32)]
    gather x1 -> x0, local copies, waits for them, and re-layouts: 6.04 us -> none  [per_device(): returned.reshape(experts_all * capacity, width)[target]]
    scatter x1 -> x0, local copies, waits for them, and re-layouts: 5.48 us -> none  [per_device(): jnp.zeros((experts_all * capacity, width), jnp.bfloat16).at[target]]
    all_to_all x1 -> x0, starting transfers between devices: 5.45 us -> none  [per_device(): lax.all_to_all(answers, ('sec', 'dev'), split_axis=0, concat_axis=0, tile...]
  transfers between devices with their start and end apart: 1 -> 0, of which waited for: 1 -> 0; matrix products, arithmetic and copies ran while one was open for 0% -> 0% of each run, Pallas kernels for 0% -> 0%
where the time goes in v1:
time: 94.3 us; the launch traced here: 94.1 us
  Pallas kernels  89.7 us (95%)
  local copies, waits for them, and re-layouts  4.37 us (5%)
    pallas_call x1, Pallas kernels, per_device(): pl.pallas_call(kernel, out_shape=jax.ShapeDtypeStruct((TOK, D), BF), in_s...  89.7 us
    unnamed x3, local copies, waits for them, and re-layouts  4.37 us

profile of v1, /device:TPU:1, one launch (start us, length us, event | category | flops | bytes accessed | tf_op | source)
XLA Modules:
  0.0 94.1 jit_solution(15974475033691697834)
XLA Ops:
  0.0 1.4 %copy.7.ids_ref = s32[32,8]{1,0:T(8,128)} copy(s32[32,8]{0,1:T(8,128)} %param.7) | data formatting | bytes 2048 | tf_op args[1]
  1.4 1.4 %copy.8.gates_ref = f32[32,8]{1,0:T(8,128)} copy(f32[32,8]{0,1:T(8,128)} %param.8) | data formatting | bytes 2048 | tf_op args[2]
  2.7 89.7 %expert_layer.1 = bf16[32,3584]{1,0:T(8,128)(2,1)} custom-call(s32[32,8]{1,0:T(8,128)} %copy.7.ids_ref, f32[32,8]{1,0:T(8,128)} %copy.8.gates_ref, bf16[32,3584]{1,0:T(8,128)(2,1)} %tok_ref.1, bf16[1,3584,1024]{2,1,0:T(8,128)(2,1)} %wg_hbm.1, bf16[1,3584,1024]{2,1,0:T(8,128)(2,1)} %wu_hbm.1, bf16[1,1024,3584]{2,1,0:T(8,128)(2,1)} %wd_hbm.1), custom_call_target="tpu_custom_call" | custom-call | flops 11274289152 | bytes 22020096 | tf_op jit(solution)/shard_map/expert_layer/pallas_call | solution.py:294
  92.4 1.6 %copy.10 = bf16[32,3584]{1,0:T(8,128)(2,1)} copy(bf16[32,3584]{1,0:T(8,128)(2,1)} %expert_layer.1) | data formatting | bytes 458752

commit v2 on v1

v2 whole, which is shorter than its diff:
```python
import jax
import jax.numpy as jnp
from jax import lax
from jax.experimental import pallas as pl
from jax.experimental.pallas import tpu as pltpu
from jax.sharding import PartitionSpec as P

MESH = pl.DeviceIdType.MESH
BF = jnp.bfloat16
F32 = jnp.float32
TOK = 32
LINE = 128
ROWS = 512
UNIT = 64
D = 3584
FF = 1024
ROUNDS = ((512, 384, 384), (384, 384, 512), (384, 384, 256))


def chunks():
    out, start = [], 0
    for widths in ROUNDS:
        row = []
        for width in widths:
            row.append((start, width))
            start += width
        out.append(row)
    return out


def coords():
    z, d = lax.axis_index("sec"), lax.axis_index("dev")
    return z, lax.div(d, 8), lax.rem(lax.div(d, 2), 4), lax.rem(d, 2)


def abc(p, zxy):
    return zxy[p], zxy[(p + 1) % 3], zxy[(p + 2) % 3]


def zxy_of(p, a, b, c):
    return ((a, b, c), (c, a, b), (b, c, a))[p]


def device_of(p, a, b, c, core):
    z, x, y = zxy_of(p, a, b, c)
    return (z, x * 8 + y * 2 + core)


def iota(shape, dim):
    return lax.broadcasted_iota(jnp.int32, shape, dim)


def dot_nt(a, b):
    return lax.dot_general(a, b, (((1,), (1,)), ((), ())), preferred_element_type=F32)


def dot(a, b):
    return jnp.dot(a, b, preferred_element_type=F32)


def eye(rows, cols):
    shape = (rows, cols)
    return (iota(shape, 0) == iota(shape, 1)).astype(F32).astype(BF)


def reorder(p):
    shape = (ROWS, ROWS)
    r = iota(shape, 0)
    slot, z, x = r & 3, lax.shift_right_logical(r, 2) & 3, lax.shift_right_logical(r, 4) & 3
    core, y = lax.shift_right_logical(r, 6) & 1, lax.shift_right_logical(r, 7)
    a, b, c = abc(p, (z, x, y))
    other = (c * 2 + core) * UNIT + b * 16 + a * 4 + slot
    return (iota(shape, 1) == other).astype(F32).astype(BF)


def wait_for(ref, sem):
    pltpu.make_async_copy(ref, ref, sem).wait()


def block(i, size):
    return pl.ds(pl.multiple_of(i * size, size), size)


def pair_table(ids_ref, gates_ref):
    ids = ids_ref[...]
    gates = gates_ref[...]
    expert = iota((128, TOK), 0)
    hits = [ids[k : k + 1, :] == expert for k in range(8)]
    named = sum(hit.astype(F32) for hit in hits)
    earlier = (iota((TOK, TOK), 0) < iota((TOK, TOK), 1)).astype(F32).astype(BF)
    slot = dot(named.astype(BF), earlier) + 1.0
    slots = [jnp.sum(jnp.where(hit, slot, 0.0), axis=0, keepdims=True) for hit in hits]
    high = gates.astype(BF).astype(F32)
    lines = [ids.astype(F32)] + slots + [high, gates - high, jnp.zeros((96, TOK), F32)]
    return dot_nt(eye(TOK, TOK), jnp.concatenate(lines, axis=0).astype(BF)).astype(BF)


def kernel(
    ids_ref, gates_ref, tok_ref, wg_hbm, wu_hbm, wd_hbm, out_ref,
    wg, wu, wd, meta, meta1, meta2, gath1, gath2, send, recv, acc_g, acc_u, hid, back, mid, mid_sum, fin,
    perm, pick, comb,
    w_sem, m1_ss, m1_rs, m2_ss, m2_rs, s1_ss, s1_rs, s2_ss, s2_rs, s3_ss, s3_rs,
    s4_ss, s4_rs, s5_ss, s5_rs, s6_ss, s6_rs,
):
    z, x, y, core = coords()
    zxy = (z, x, y)
    table = chunks()
    every = [(r, p, start, width) for r, row in enumerate(table) for p, (start, width) in enumerate(row)]

    barrier = pltpu.get_barrier_semaphore()
    for p in range(3):
        a, b, c = abc(p, zxy)
        for n in (1, 2, 3):
            for other in (0, 1):
                pl.semaphore_signal(
                    barrier, inc=1, device_id=device_of(p, a, b, lax.rem(c + n, 4), lax.rem(core + other, 2)),
                    device_id_type=MESH,
                )
    pl.semaphore_signal(barrier, inc=1, device_id=device_of(0, z, x, y, 1 - core), device_id_type=MESH)

    weights = [
        pltpu.make_async_copy(src.at[0], dst, w_sem.at[i])
        for i, (src, dst) in enumerate(((wg_hbm, wg), (wu_hbm, wu), (wd_hbm, wd)))
    ]
    for copy in weights:
        copy.start()

    meta[...] = pair_table(ids_ref, gates_ref)
    pl.semaphore_wait(barrier, 19)

    def along_a(p, src, dst, ss, rs):
        a, b, c = abc(p, zxy)
        for n in (1, 3, 2):
            to = lax.rem(a + n, 4)
            pltpu.make_async_remote_copy(
                src(to), dst, ss, rs, device_id=device_of(p, to, b, c, core), device_id_type=MESH
            ).start()

    def along_b(p, src, dst, ss, rs):
        a, b, c = abc(p, zxy)
        for n in (1, 3, 2):
            to = lax.rem(b + n, 4)
            pltpu.make_async_remote_copy(
                src(to), dst, ss, rs, device_id=device_of(p, a, to, c, core), device_id_type=MESH
            ).start()

    def along_c(p, src, dst, cols, ss, rs):
        a, b, c = abc(p, zxy)
        mine = block(c * 2 + core, UNIT)
        for n in (1, 3, 2, 0):
            for m in (0, 1):
                if n == 0 and m == 0:
                    continue
                to, to_core = lax.rem(c + n, 4), lax.rem(core + m, 2)
                pltpu.make_async_remote_copy(
                    src.at[block(to * 2 + to_core, UNIT), cols], dst.at[mine, cols], ss, rs,
                    device_id=device_of(p, a, b, to, to_core), device_id_type=MESH,
                ).start()
        pltpu.make_async_copy(src.at[mine, cols], dst.at[mine, cols], rs).start()

    for p in range(3):
        mine = block(zxy[p], TOK)
        along_a(p, lambda to: meta, meta1.at[p, mine], m1_ss, m1_rs.at[p])
        pltpu.make_async_copy(meta, meta1.at[p, mine], m1_rs.at[p]).start()
    for r, p, start, width in every:
        cols, mine = pl.ds(start, width), block(zxy[p], TOK)
        along_a(p, lambda to: tok_ref.at[:, cols], gath1.at[mine, cols], s1_ss, s1_rs.at[r, p])
        pltpu.make_async_copy(tok_ref.at[:, cols], gath1.at[mine, cols], s1_rs.at[r, p]).start()
    for p in range(3):
        mine = block(zxy[(p + 1) % 3], LINE)
        wait_for(meta1.at[p], m1_rs.at[p])
        along_b(p, lambda to: meta1.at[p], meta2.at[p, mine], m2_ss, m2_rs.at[p])
        pltpu.make_async_copy(meta1.at[p], meta2.at[p, mine], m2_rs.at[p]).start()
    for r, p, start, width in every:
        cols, mine = pl.ds(start, width), block(zxy[(p + 1) % 3], LINE)
        wait_for(gath1.at[:, cols], s1_rs.at[r, p])
        along_b(p, lambda to: gath1.at[:, cols], gath2.at[mine, cols], s2_ss, s2_rs.at[r, p])
        pltpu.make_async_copy(gath1.at[:, cols], gath2.at[mine, cols], s2_rs.at[r, p]).start()

    def tables(p, weighted):
        a, b, c = abc(p, zxy)
        lanes = dot_nt(eye(TOK, 128), meta2[p])
        ids, slots, high, low = (lanes[8 * i : 8 * i + 8] for i in range(4))

        def per_unit(values):
            out = []
            for u in range(8):
                to_z, to_x, to_y = zxy_of(p, a, b, u // 2)
                expert = to_z * 32 + to_x * 8 + to_y * 2 + u % 2
                hit = ids == expert.astype(F32)
                row = jnp.sum(jnp.where(hit, values, 0.0), axis=0, keepdims=True)
                out.append(jnp.broadcast_to(row, (UNIT, ROWS)))
            return jnp.concatenate(out, axis=0)

        rows, cols = iota((ROWS, ROWS), 0), iota((ROWS, ROWS), 1)
        want = ((rows & 3) + 1).astype(F32)
        same = (lax.shift_right_logical(rows, 2) & 15) == lax.shift_right_logical(cols, 5)
        hit = (per_unit(slots) == want) & same
        if weighted:
            comb[p, 0:ROWS] = jnp.where(hit, per_unit(high), 0.0).T.astype(BF)
            comb[p, ROWS : 2 * ROWS] = jnp.where(hit, per_unit(low), 0.0).T.astype(BF)
        else:
            pick[p] = jnp.where(hit, 1.0, 0.0).astype(BF)

    for p in range(3):
        wait_for(meta2.at[p], m2_rs.at[p])
        tables(p, False)
    for r, p, start, width in every:
        cols = pl.ds(start, width)
        wait_for(gath2.at[:, cols], s2_rs.at[r, p])
        send[:, cols] = dot(pick[p], gath2[:, cols]).astype(BF)
        along_c(p, send, recv, cols, s3_ss, s3_rs.at[r, p])

    for p in (1, 2):
        perm[p - 1] = reorder(p)
    for p in range(3):
        tables(p, True)
    for copy in weights:
        copy.wait()

    for r, row in enumerate(table):
        for p, (start, width) in enumerate(row):
            cols = pl.ds(start, width)
            wait_for(recv.at[:, cols], s3_rs.at[r, p])
            if p > 0:
                recv[:, cols] = dot(perm[p - 1], recv[:, cols]).astype(BF)
        first = row[0][0]
        depth = pl.ds(first, sum(width for _, width in row))

        def body(i, carry, r=r, depth=depth):
            at = block(i, 256)
            g = dot(recv[:, depth], wg[depth, at])
            u = dot(recv[:, depth], wu[depth, at])
            if r > 0:
                g = g + acc_g[:, at]
                u = u + acc_u[:, at]
            if r < len(table) - 1:
                acc_g[:, at] = g
                acc_u[:, at] = u
            else:
                hid[0, :, at] = (g / (1.0 + jnp.exp(-g)) * u).astype(BF)
            return carry

        lax.fori_loop(0, FF // 256, body, 0)
    for p in (1, 2):
        hid[p] = lax.dot_general(
            perm[p - 1], hid[0], (((0,), (0,)), ((), ())), preferred_element_type=F32
        ).astype(BF)

    wait_for(send.at[pl.ds(0, ROWS - UNIT)], s3_ss)
    for r, p, start, width in every:
        cols = pl.ds(start, width)
        send[:, cols] = dot(hid[p], wd[:, cols]).astype(BF)
        along_c(p, send, back, cols, s4_ss, s4_rs.at[r, p])
    for r, p, start, width in every:
        cols, b = pl.ds(start, width), zxy[(p + 1) % 3]
        wait_for(back.at[:, cols], s4_rs.at[r, p])
        both = dot(comb[p], back[:, cols])
        recv[:, cols] = (both[0:ROWS] + both[ROWS : 2 * ROWS]).astype(BF)
        along_b(p, lambda to: recv.at[block(to, LINE), cols], mid.at[b, :, cols], s5_ss, s5_rs.at[r, p])
        pltpu.make_async_copy(recv.at[block(b, LINE), cols], mid.at[b, :, cols], s5_rs.at[r, p]).start()
    for r, p, start, width in every:
        cols, a = pl.ds(start, width), zxy[p]
        wait_for(mid.at[:, :, cols], s5_rs.at[r, p])
        mid_sum[:, cols] = sum(mid[k, :, cols].astype(F32) for k in range(4)).astype(BF)
        along_a(p, lambda to: mid_sum.at[block(to, TOK), cols], fin.at[a, :, cols], s6_ss, s6_rs.at[r, p])
        pltpu.make_async_copy(mid_sum.at[block(a, TOK), cols], fin.at[a, :, cols], s6_rs.at[r, p]).start()
    for r, p, start, width in every:
        cols = pl.ds(start, width)
        wait_for(fin.at[:, :, cols], s6_rs.at[r, p])
        out_ref[:, cols] = sum(fin[k, :, cols].astype(F32) for k in range(4)).astype(BF)

    wait_for(meta1.at[:, pl.ds(0, 96)], m1_ss)
    wait_for(meta2.at[:, pl.ds(0, 384)], m2_ss)
    wait_for(gath1.at[pl.ds(0, 96)], s1_ss)
    wait_for(gath2.at[pl.ds(0, 384)], s2_ss)
    wait_for(send.at[pl.ds(0, ROWS - UNIT)], s4_ss)
    wait_for(recv.at[pl.ds(0, 384)], s5_ss)
    wait_for(mid_sum.at[pl.ds(0, 96)], s6_ss)


def per_device(tokens, expert_ids, gate_values, w_gate, w_up, w_down):
    n = len(ROUNDS)
    dma = pltpu.SemaphoreType.DMA
    vmem = pl.BlockSpec(memory_space=pltpu.VMEM)
    hbm = pl.BlockSpec(memory_space=pl.ANY)
    return pl.pallas_call(
        kernel,
        out_shape=jax.ShapeDtypeStruct((TOK, D), BF),
        in_specs=[vmem, vmem, vmem, hbm, hbm, hbm],
        out_specs=vmem,
        scratch_shapes=[
            pltpu.VMEM((D, FF), BF),
            pltpu.VMEM((D, FF), BF),
            pltpu.VMEM((FF, D), BF),
            pltpu.VMEM((TOK, 128), BF),
            pltpu.VMEM((3, LINE, 128), BF),
            pltpu.VMEM((3, ROWS, 128), BF),
            pltpu.VMEM((LINE, D), BF),
            pltpu.VMEM((ROWS, D), BF),
            pltpu.VMEM((ROWS, D), BF),
            pltpu.VMEM((ROWS, D), BF),
            pltpu.VMEM((ROWS, FF), F32),
            pltpu.VMEM((ROWS, FF), F32),
            pltpu.VMEM((3, ROWS, FF), BF),
            pltpu.VMEM((ROWS, D), BF),
            pltpu.VMEM((4, LINE, D), BF),
            pltpu.VMEM((LINE, D), BF),
            pltpu.VMEM((4, TOK, D), BF),
            pltpu.VMEM((2, ROWS, ROWS), BF),
            pltpu.VMEM((3, ROWS, ROWS), BF),
            pltpu.VMEM((3, 2 * ROWS, ROWS), BF),
            dma((3,)),
            dma, dma((3,)),
            dma, dma((3,)),
            dma, dma((n, 3)),
            dma, dma((n, 3)),
            dma, dma((n, 3)),
            dma, dma((n, 3)),
            dma, dma((n, 3)),
            dma, dma((n, 3)),
        ],
        compiler_params=pltpu.CompilerParams(
            collective_id=0, has_side_effects=True, vmem_limit_bytes=62 * 2**20
        ),
        cost_estimate=pl.CostEstimate(
            flops=6 * ROWS * D * FF, bytes_accessed=6 * D * FF, transcendentals=ROWS * FF
        ),
        name="expert_layer",
    )(expert_ids.T, gate_values.T, tokens, w_gate, w_up, w_down)


def solution(mesh):
    rows = P(("sec", "dev"), None)
    experts = P(("sec", "dev"), None, None)
    return jax.shard_map(
        per_device,
        mesh=mesh,
        in_specs=(rows, rows, rows, experts, experts, experts),
        out_specs=rows,
        check_vma=False,
    )
```

time: 94.3 us -> 88.2 us (0.935)
  Pallas kernels: 89.7 us -> 86.4 us
  local copies, waits for them, and re-layouts: 4.37 us -> 1.64 us
    pallas_call x1, Pallas kernels: 89.7 us -> 86.4 us  [per_device(): pl.pallas_call(kernel, out_shape=jax.ShapeDtypeStruct((TOK, D), BF), in_s...]
    unnamed x3 -> x1, local copies, waits for them, and re-layouts: 4.37 us -> 1.64 us
where the time goes in v2:
time: 88.2 us; the launch traced here: 88.1 us
  Pallas kernels  86.4 us (98%)
  local copies, waits for them, and re-layouts  1.64 us (2%)
    pallas_call x1, Pallas kernels, per_device(): pl.pallas_call(kernel, out_shape=jax.ShapeDtypeStruct((TOK, D), BF), in_s...  86.4 us

profile of v2, /device:TPU:1, one launch (start us, length us, event | category | flops | bytes accessed | tf_op | source)
XLA Modules:
  0.0 88.1 jit_solution(17955005809534954496)
XLA Ops:
  0.0 86.4 %expert_layer.1 = bf16[32,3584]{1,0:T(8,128)(2,1)} custom-call(s32[8,32]{1,0:T(8,128)} %bitcast.2, f32[8,32]{1,0:T(8,128)} %bitcast.3, bf16[32,3584]{1,0:T(8,128)(2,1)} %tok_ref.1, bf16[1,3584,1024]{2,1,0:T(8,128)(2,1)} %wg_hbm.1, bf16[1,3584,1024]{2,1,0:T(8,128)(2,1)} %wu_hbm.1, bf16[1,1024,3584]{2,1,0:T(8,128)(2,1)} %wd_hbm.1), custom_call_target="tpu_custom_call" | custom-call | flops 11274289152 | bytes 22020096 | tf_op jit(solution)/shard_map/expert_layer/pallas_call | solution.py:287
  86.5 1.6 %copy.8 = bf16[32,3584]{1,0:T(8,128)(2,1)} copy(bf16[32,3584]{1,0:T(8,128)(2,1)} %expert_layer.1) | data formatting | bytes 458752

commit v3 on v2

--- a/solution.py
+++ b/solution.py
@@ -14,7 +14,7 @@
 UNIT = 64
 D = 3584
 FF = 1024
-ROUNDS = ((512, 384, 384), (384, 384, 512), (384, 384, 256))
+ROUNDS = ((256, 256, 256), (256, 256, 256), (256, 256, 256), (256, 256, 256), (256, 128, 128))
 
 
 def chunks():
@@ -90,22 +90,25 @@
     earlier = (iota((TOK, TOK), 0) < iota((TOK, TOK), 1)).astype(F32).astype(BF)
     slot = dot(named.astype(BF), earlier) + 1.0
     slots = [jnp.sum(jnp.where(hit, slot, 0.0), axis=0, keepdims=True) for hit in hits]
-    high = gates.astype(BF).astype(F32)
-    lines = [ids.astype(F32)] + slots + [high, gates - high, jnp.zeros((96, TOK), F32)]
+    lines = [ids.astype(F32)] + slots + [gates, jnp.zeros((104, TOK), F32)]
     return dot_nt(eye(TOK, TOK), jnp.concatenate(lines, axis=0).astype(BF)).astype(BF)
 
 
 def kernel(
     ids_ref, gates_ref, tok_ref, wg_hbm, wu_hbm, wd_hbm, out_ref,
-    wg, wu, wd, meta, meta1, meta2, gath1, gath2, send, recv, acc_g, acc_u, hid, back, mid, mid_sum, fin,
+    wg, wu, wd, meta, meta1, meta2, gath1, gath2, send, recv, acc_g, acc_u, hid, back, far, mid, mid_sum, fin,
     perm, pick, comb,
     w_sem, m1_ss, m1_rs, m2_ss, m2_rs, s1_ss, s1_rs, s2_ss, s2_rs, s3_ss, s3_rs,
-    s4_ss, s4_rs, s5_ss, s5_rs, s6_ss, s6_rs,
+    s4_ss, s4_rs, s5_ss, s5_rs, s6_ss, s6_rs, s7_ss, s7_rs, s8_ss, s8_rs,
 ):
     z, x, y, core = coords()
     zxy = (z, x, y)
     table = chunks()
-    every = [(r, p, start, width) for r, row in enumerate(table) for p, (start, width) in enumerate(row)]
+    rounds = len(table)
+
+    def parts_of(r):
+        return [(p, start, pl.ds(start, width)) for p, (start, width) in enumerate(table[r])]
+
 
     barrier = pltpu.get_barrier_semaphore()
     for p in range(3):
@@ -126,6 +129,8 @@
         copy.start()
 
     meta[...] = pair_table(ids_ref, gates_ref)
+    for p in (1, 2):
+        perm[p - 1] = reorder(p)
     pl.semaphore_wait(barrier, 19)
 
     def along_a(p, src, dst, ss, rs):
@@ -136,13 +141,11 @@
                 src(to), dst, ss, rs, device_id=device_of(p, to, b, c, core), device_id_type=MESH
             ).start()
 
-    def along_b(p, src, dst, ss, rs):
-        a, b, c = abc(p, zxy)
-        for n in (1, 3, 2):
-            to = lax.rem(b + n, 4)
-            pltpu.make_async_remote_copy(
-                src(to), dst, ss, rs, device_id=device_of(p, a, to, c, core), device_id_type=MESH
-            ).start()
+    def next_b(p, step, src, dst, ss, rs):
+        a, b, c = abc(p, zxy)
+        pltpu.make_async_remote_copy(
+            src, dst, ss, rs, device_id=device_of(p, a, lax.rem(b + step, 4), c, core), device_id_type=MESH
+        ).start()
 
     def along_c(p, src, dst, cols, ss, rs):
         a, b, c = abc(p, zxy)
@@ -162,25 +165,38 @@
         mine = block(zxy[p], TOK)
         along_a(p, lambda to: meta, meta1.at[p, mine], m1_ss, m1_rs.at[p])
         pltpu.make_async_copy(meta, meta1.at[p, mine], m1_rs.at[p]).start()
-    for r, p, start, width in every:
-        cols, mine = pl.ds(start, width), block(zxy[p], TOK)
-        along_a(p, lambda to: tok_ref.at[:, cols], gath1.at[mine, cols], s1_ss, s1_rs.at[r, p])
-        pltpu.make_async_copy(tok_ref.at[:, cols], gath1.at[mine, cols], s1_rs.at[r, p]).start()
+    for r in range(rounds):
+        for p, start, cols in parts_of(r):
+            mine = block(zxy[p], TOK)
+            along_a(p, lambda to: tok_ref.at[:, cols], gath1.at[mine, cols], s1_ss, s1_rs.at[r, p])
+            pltpu.make_async_copy(tok_ref.at[:, cols], gath1.at[mine, cols], s1_rs.at[r, p]).start()
     for p in range(3):
-        mine = block(zxy[(p + 1) % 3], LINE)
+        b = zxy[(p + 1) % 3]
         wait_for(meta1.at[p], m1_rs.at[p])
-        along_b(p, lambda to: meta1.at[p], meta2.at[p, mine], m2_ss, m2_rs.at[p])
-        pltpu.make_async_copy(meta1.at[p], meta2.at[p, mine], m2_rs.at[p]).start()
-    for r, p, start, width in every:
-        cols, mine = pl.ds(start, width), block(zxy[(p + 1) % 3], LINE)
-        wait_for(gath1.at[:, cols], s1_rs.at[r, p])
-        along_b(p, lambda to: gath1.at[:, cols], gath2.at[mine, cols], s2_ss, s2_rs.at[r, p])
-        pltpu.make_async_copy(gath1.at[:, cols], gath2.at[mine, cols], s2_rs.at[r, p]).start()
+        for n in (1, 3, 2):
+            next_b(p, n, meta1.at[p], meta2.at[p, block(b, LINE)], m2_ss, m2_rs.at[p])
+        pltpu.make_async_copy(meta1.at[p], meta2.at[p, block(b, LINE)], m2_rs.at[p]).start()
+
+    def to_neighbours(r):
+        for p, start, cols in parts_of(r):
+            mine = block(zxy[(p + 1) % 3], LINE)
+            wait_for(gath1.at[:, cols], s1_rs.at[r, p])
+            next_b(p, 1, gath1.at[:, cols], gath2.at[mine, cols], s2_ss, s2_rs.at[r, p, 0])
+            next_b(p, 3, gath1.at[:, cols], gath2.at[mine, cols], s2_ss, s2_rs.at[r, p, 1])
+            pltpu.make_async_copy(gath1.at[:, cols], gath2.at[mine, cols], s7_rs.at[r, p]).start()
+
+    def pass_on(r):
+        for p, start, cols in parts_of(r):
+            b = zxy[(p + 1) % 3]
+            for side, step, source in ((0, 1, lax.rem(b + 3, 4)), (1, 3, lax.rem(b + 1, 4))):
+                wait_for(gath2.at[block(source, LINE), cols], s2_rs.at[r, p, side])
+                half = gath2.at[block(source * 2 + side, 64), cols]
+                next_b(p, step, half, half, s7_ss, s7_rs.at[r, p])
 
     def tables(p, weighted):
         a, b, c = abc(p, zxy)
         lanes = dot_nt(eye(TOK, 128), meta2[p])
-        ids, slots, high, low = (lanes[8 * i : 8 * i + 8] for i in range(4))
+        ids, slots, gates = (lanes[8 * i : 8 * i + 8] for i in range(3))
 
         def per_unit(values):
             out = []
@@ -197,85 +213,103 @@
         same = (lax.shift_right_logical(rows, 2) & 15) == lax.shift_right_logical(cols, 5)
         hit = (per_unit(slots) == want) & same
         if weighted:
-            comb[p, 0:ROWS] = jnp.where(hit, per_unit(high), 0.0).T.astype(BF)
-            comb[p, ROWS : 2 * ROWS] = jnp.where(hit, per_unit(low), 0.0).T.astype(BF)
+            comb[p] = jnp.where(hit, per_unit(gates), 0.0).T.astype(BF)
         else:
             pick[p] = jnp.where(hit, 1.0, 0.0).astype(BF)
 
-    for p in range(3):
-        wait_for(meta2.at[p], m2_rs.at[p])
-        tables(p, False)
-    for r, p, start, width in every:
-        cols = pl.ds(start, width)
-        wait_for(gath2.at[:, cols], s2_rs.at[r, p])
-        send[:, cols] = dot(pick[p], gath2[:, cols]).astype(BF)
-        along_c(p, send, recv, cols, s3_ss, s3_rs.at[r, p])
-
-    for p in (1, 2):
-        perm[p - 1] = reorder(p)
-    for p in range(3):
-        tables(p, True)
-    for copy in weights:
-        copy.wait()
-
-    for r, row in enumerate(table):
-        for p, (start, width) in enumerate(row):
-            cols = pl.ds(start, width)
+    def slots_out(r):
+        for p, start, cols in parts_of(r):
+            if r == 0:
+                wait_for(meta2.at[p], m2_rs.at[p])
+                tables(p, False)
+            wait_for(gath2.at[pl.ds(0, 2 * LINE), cols], s7_rs.at[r, p])
+            send[:, cols] = dot(pick[p], gath2[:, cols]).astype(BF)
+            along_c(p, send, recv, cols, s3_ss, s3_rs.at[r, p])
+        if r < 3:
+            tables(r, True)
+
+    def multiply(r):
+        if r == 0:
+            for copy in weights:
+                copy.wait()
+        for p, start, cols in parts_of(r):
             wait_for(recv.at[:, cols], s3_rs.at[r, p])
             if p > 0:
                 recv[:, cols] = dot(perm[p - 1], recv[:, cols]).astype(BF)
-        first = row[0][0]
-        depth = pl.ds(first, sum(width for _, width in row))
-
-        def body(i, carry, r=r, depth=depth):
-            at = block(i, 256)
+        depth = pl.ds(table[r][0][0], sum(width for _, width in table[r]))
+        for i in range(FF // 512):
+            at = pl.ds(i * 512, 512)
             g = dot(recv[:, depth], wg[depth, at])
             u = dot(recv[:, depth], wu[depth, at])
             if r > 0:
                 g = g + acc_g[:, at]
                 u = u + acc_u[:, at]
-            if r < len(table) - 1:
+            if r < rounds - 1:
                 acc_g[:, at] = g
                 acc_u[:, at] = u
             else:
                 hid[0, :, at] = (g / (1.0 + jnp.exp(-g)) * u).astype(BF)
-            return carry
-
-        lax.fori_loop(0, FF // 256, body, 0)
-    for p in (1, 2):
-        hid[p] = lax.dot_general(
-            perm[p - 1], hid[0], (((0,), (0,)), ((), ())), preferred_element_type=F32
-        ).astype(BF)
-
+
+    def answers_out(r):
+        for p, start, cols in parts_of(r):
+            if r == 0 and p > 0:
+                hid[p] = lax.dot_general(
+                    perm[p - 1], hid[0], (((0,), (0,)), ((), ())), preferred_element_type=F32
+                ).astype(BF)
+            send[:, cols] = dot(hid[p], wd[:, cols]).astype(BF)
+            along_c(p, send, back, cols, s4_ss, s4_rs.at[r, p])
+
+    def sums_out(r):
+        for p, start, cols in parts_of(r):
+            across = lax.rem(zxy[(p + 1) % 3] + 2, 4)
+            wait_for(back.at[:, cols], s4_rs.at[r, p])
+            recv[:, cols] = dot(comb[p], back[:, cols]).astype(BF)
+            for side, step in ((0, 1), (1, 3)):
+                half = recv.at[block(across * 2 + side, 64), cols]
+                next_b(p, step, half, far.at[side, :, cols], s5_ss, s5_rs.at[r, p])
+
+    def sums_on(r):
+        for p, start, cols in parts_of(r):
+            b = zxy[(p + 1) % 3]
+            wait_for(far.at[:, :, cols], s5_rs.at[r, p])
+            for side, step in ((0, 1), (1, 3)):
+                to = lax.rem(b + step, 4)
+                half = block(to * 2 + side, 64)
+                recv[half, cols] = (recv[half, cols].astype(F32) + far[side, :, cols].astype(F32)).astype(BF)
+                next_b(p, step, recv.at[block(to, LINE), cols], mid.at[side, :, cols], s8_ss, s8_rs.at[r, p])
+
+    def sums_home(r):
+        for p, start, cols in parts_of(r):
+            a, b, _ = abc(p, zxy)
+            wait_for(mid.at[:, :, cols], s8_rs.at[r, p])
+            total = recv[block(b, LINE), cols].astype(F32)
+            mid_sum[:, cols] = (total + mid[0, :, cols].astype(F32) + mid[1, :, cols].astype(F32)).astype(BF)
+            along_a(p, lambda to: mid_sum.at[block(to, TOK), cols], fin.at[a, :, cols], s6_ss, s6_rs.at[r, p])
+            pltpu.make_async_copy(mid_sum.at[block(a, TOK), cols], fin.at[a, :, cols], s6_rs.at[r, p]).start()
+
+    def finish(r):
+        for p, start, cols in parts_of(r):
+            wait_for(fin.at[:, :, cols], s6_rs.at[r, p])
+            out_ref[:, cols] = sum(fin[k, :, cols].astype(F32) for k in range(4)).astype(BF)
+
+    def staggered(*steps):
+        for i in range(rounds + max(lag for _, lag in steps)):
+            for step, lag in steps:
+                if 0 <= i - lag < rounds:
+                    step(i - lag)
+
+    staggered((to_neighbours, 0), (pass_on, 2), (slots_out, 4), (multiply, 6))
     wait_for(send.at[pl.ds(0, ROWS - UNIT)], s3_ss)
-    for r, p, start, width in every:
-        cols = pl.ds(start, width)
-        send[:, cols] = dot(hid[p], wd[:, cols]).astype(BF)
-        along_c(p, send, back, cols, s4_ss, s4_rs.at[r, p])
-    for r, p, start, width in every:
-        cols, b = pl.ds(start, width), zxy[(p + 1) % 3]
-        wait_for(back.at[:, cols], s4_rs.at[r, p])
-        both = dot(comb[p], back[:, cols])
-        recv[:, cols] = (both[0:ROWS] + both[ROWS : 2 * ROWS]).astype(BF)
-        along_b(p, lambda to: recv.at[block(to, LINE), cols], mid.at[b, :, cols], s5_ss, s5_rs.at[r, p])
-        pltpu.make_async_copy(recv.at[block(b, LINE), cols], mid.at[b, :, cols], s5_rs.at[r, p]).start()
-    for r, p, start, width in every:
-        cols, a = pl.ds(start, width), zxy[p]
-        wait_for(mid.at[:, :, cols], s5_rs.at[r, p])
-        mid_sum[:, cols] = sum(mid[k, :, cols].astype(F32) for k in range(4)).astype(BF)
-        along_a(p, lambda to: mid_sum.at[block(to, TOK), cols], fin.at[a, :, cols], s6_ss, s6_rs.at[r, p])
-        pltpu.make_async_copy(mid_sum.at[block(a, TOK), cols], fin.at[a, :, cols], s6_rs.at[r, p]).start()
-    for r, p, start, width in every:
-        cols = pl.ds(start, width)
-        wait_for(fin.at[:, :, cols], s6_rs.at[r, p])
-        out_ref[:, cols] = sum(fin[k, :, cols].astype(F32) for k in range(4)).astype(BF)
+    staggered((answers_out, 0), (sums_out, 2), (sums_on, 4), (sums_home, 6), (finish, 8))
 
     wait_for(meta1.at[:, pl.ds(0, 96)], m1_ss)
     wait_for(meta2.at[:, pl.ds(0, 384)], m2_ss)
     wait_for(gath1.at[pl.ds(0, 96)], s1_ss)
-    wait_for(gath2.at[pl.ds(0, 384)], s2_ss)
+    wait_for(gath2.at[pl.ds(0, 256)], s2_ss)
+    wait_for(gath2.at[pl.ds(0, 128)], s7_ss)
     wait_for(send.at[pl.ds(0, ROWS - UNIT)], s4_ss)
-    wait_for(recv.at[pl.ds(0, 384)], s5_ss)
+    wait_for(recv.at[pl.ds(0, 128)], s5_ss)
+    wait_for(recv.at[pl.ds(0, 256)], s8_ss)
     wait_for(mid_sum.at[pl.ds(0, 96)], s6_ss)
 
 
@@ -304,15 +338,18 @@
             pltpu.VMEM((ROWS, FF), F32),
             pltpu.VMEM((3, ROWS, FF), BF),
             pltpu.VMEM((ROWS, D), BF),
-            pltpu.VMEM((4, LINE, D), BF),
+            pltpu.VMEM((2, 64, D), BF),
+            pltpu.VMEM((2, LINE, D), BF),
             pltpu.VMEM((LINE, D), BF),
             pltpu.VMEM((4, TOK, D), BF),
             pltpu.VMEM((2, ROWS, ROWS), BF),
             pltpu.VMEM((3, ROWS, ROWS), BF),
-            pltpu.VMEM((3, 2 * ROWS, ROWS), BF),
+            pltpu.VMEM((3, ROWS, ROWS), BF),
             dma((3,)),
             dma, dma((3,)),
             dma, dma((3,)),
+            dma, dma((n, 3)),
+            dma, dma((n, 3, 2)),
             dma, dma((n, 3)),
             dma, dma((n, 3)),
             dma, dma((n, 3)),

time: 88.2 us -> 81.1 us (0.920)
  Pallas kernels: 86.4 us -> 79.1 us
    pallas_call x1, Pallas kernels: 86.4 us -> 79.1 us  [per_device(): pl.pallas_call(kernel, out_shape=jax.ShapeDtypeStruct((TOK, D), BF), in_s...]
where the time goes in v3:
time: 81.1 us; the launch traced here: 80.8 us
  Pallas kernels  79.1 us (98%)
  local copies, waits for them, and re-layouts  1.64 us (2%)
    pallas_call x1, Pallas kernels, per_device(): pl.pallas_call(kernel, out_shape=jax.ShapeDtypeStruct((TOK, D), BF), in_s...  79.1 us
    unnamed x1, local copies, waits for them, and re-layouts  1.64 us

profile of v3, /device:TPU:1, one launch (start us, length us, event | category | flops | bytes accessed | tf_op | source)
XLA Modules:
  0.0 80.8 jit_solution(8039279452463969580)
XLA Ops:
  0.0 79.1 %expert_layer.1 = bf16[32,3584]{1,0:T(8,128)(2,1)} custom-call(s32[8,32]{1,0:T(8,128)} %bitcast.2, f32[8,32]{1,0:T(8,128)} %bitcast.3, bf16[32,3584]{1,0:T(8,128)(2,1)} %tok_ref.1, bf16[1,3584,1024]{2,1,0:T(8,128)(2,1)} %wg_hbm.1, bf16[1,3584,1024]{2,1,0:T(8,128)(2,1)} %wu_hbm.1, bf16[1,1024,3584]{2,1,0:T(8,128)(2,1)} %wd_hbm.1), custom_call_target="tpu_custom_call" | custom-call | flops 11274289152 | bytes 22020096 | tf_op jit(solution)/shard_map/expert_layer/pallas_call | solution.py:321
  79.1 1.6 %copy.8 = bf16[32,3584]{1,0:T(8,128)(2,1)} copy(bf16[32,3584]{1,0:T(8,128)(2,1)} %expert_layer.1) | data formatting | bytes 458752

commit v4 on v3

--- a/solution.py
+++ b/solution.py
@@ -14,7 +14,7 @@
 UNIT = 64
 D = 3584
 FF = 1024
-ROUNDS = ((256, 256, 256), (256, 256, 256), (256, 256, 256), (256, 256, 256), (256, 128, 128))
+ROUNDS = ((256, 256, 256), (512, 256, 256), (256, 384, 384), (256, 256, 256))
 
 
 def chunks():

time: 81.1 us -> 80.5 us (level)
  no operation moved by 1% of the time
where the time goes in v4:
time: 80.5 us; the launch traced here: 80.1 us
  Pallas kernels  78.4 us (97%)
  local copies, waits for them, and re-layouts  1.64 us (2%)
    pallas_call x1, Pallas kernels, per_device(): pl.pallas_call(kernel, out_shape=jax.ShapeDtypeStruct((TOK, D), BF), in_s...  78.4 us
    unnamed x1, local copies, waits for them, and re-layouts  1.64 us

profile of v4, /device:TPU:1, one launch (start us, length us, event | category | flops | bytes accessed | tf_op | source)
XLA Modules:
  0.0 80.1 jit_solution(18179735722294931730)
XLA Ops:
  0.0 78.4 %expert_layer.1 = bf16[32,3584]{1,0:T(8,128)(2,1)} custom-call(s32[8,32]{1,0:T(8,128)} %bitcast.2, f32[8,32]{1,0:T(8,128)} %bitcast.3, bf16[32,3584]{1,0:T(8,128)(2,1)} %tok_ref.1, bf16[1,3584,1024]{2,1,0:T(8,128)(2,1)} %wg_hbm.1, bf16[1,3584,1024]{2,1,0:T(8,128)(2,1)} %wu_hbm.1, bf16[1,1024,3584]{2,1,0:T(8,128)(2,1)} %wd_hbm.1), custom_call_target="tpu_custom_call" | custom-call | flops 11274289152 | bytes 22020096 | tf_op jit(solution)/shard_map/expert_layer/pallas_call | solution.py:321
  78.4 1.6 %copy.8 = bf16[32,3584]{1,0:T(8,128)(2,1)} copy(bf16[32,3584]{1,0:T(8,128)(2,1)} %expert_layer.1) | data formatting | bytes 458752
